TPU v7x, 128 devices: a whole 4x4x4 slice. The times are simulated.
128 devices in a mesh: seq: 32 (over y, x_hi, z), dp: 4 (over x_lo, core).
Axes of the slice: x: 4 (x_hi: 2, x_lo: 2; x = x_hi * 2 + x_lo), y: 4, z: 4, core: 2. Of those that a mesh axis runs over, the one named last changes fastest.
Arguments:
- spectra_in: bfloat16 [24, 2048, 768], P('dp', 'seq'), may hold values from -6 to 6
- cotangent: bfloat16 [24, 2048, 768], P('dp', 'seq'), may hold values from -6 to 6
- tok_in_w: bfloat16 [2048, 1024], P('seq'), may hold values from -0.125 to 0.125
- tok_out_w: bfloat16 [2048, 1024], P('seq'), may hold values from -0.1875 to 0.1875
- ch_in_w: bfloat16 [1536, 768], replicated, may hold values from -0.21875 to 0.21875
- ch_out_w: bfloat16 [1536, 768], replicated, may hold values from -0.15625 to 0.15625
Outputs:
- grad_input: bfloat16 [24, 2048, 768], P('dp', 'seq')
- grad_tok_in: float32 [2048, 1024], P(('seq', 'dp'))
- grad_tok_out: float32 [2048, 1024], P(('seq', 'dp'))
- grad_ch_in: float32 [1536, 768], P(('seq', 'dp'))
- grad_ch_out: float32 [1536, 768], P(('seq', 'dp'))
All inputs are finite; a program needn't handle non-finite values.
Results may differ from a plain program's by a relative error of at most 0.012.
Values may be sent and summed in bfloat16 or wider, within the bound.
A program may use at most 192 MiB of HBM per device.

v0:
```python
import math
import types

import jax
import jax.numpy as jnp
from jax import lax
from jax.experimental import pallas as pl
from jax.experimental.pallas import tpu as pltpu
from jax.sharding import PartitionSpec as P

BF = jnp.bfloat16
F32 = jnp.float32
MESH = pl.DeviceIdType.MESH
ANY = pl.BlockSpec(memory_space=pl.ANY)
LANES = 128


def normalize(values):
    center = values - jnp.mean(values, axis=-1, keepdims=True)
    inv_scale = lax.rsqrt(jnp.mean(center * center, axis=-1, keepdims=True) + 1e-05)
    return (center * inv_scale, inv_scale)


def norm_back(unit, inv_scale, upstream):
    first = jnp.mean(upstream, axis=-1, keepdims=True)
    second = jnp.mean(upstream * unit, axis=-1, keepdims=True)
    return inv_scale * (upstream - first - unit * second)


def gelu_pair(values):
    factor = math.sqrt(2.0 / math.pi)
    inner = factor * (values + 0.044715 * values * values * values)
    tangent = jnp.tanh(inner)
    result = 0.5 * values * (1.0 + tangent)
    slope = 0.5 * (1.0 + tangent) + 0.5 * values * (1.0 - tangent * tangent) * factor * (
        1.0 + 3.0 * 0.044715 * values * values
    )
    return (result, slope)


class Here:
    def __init__(self):
        self.q = lax.axis_index("seq")
        self.d = lax.axis_index("dp")
        self.y = self.q // 8
        self.xh = (self.q // 4) % 2
        self.z = self.q % 4
        self.xl = self.d // 2
        self.c = self.d % 2
        self.x = self.xh * 2 + self.xl

    def at(self, x=None, y=None, z=None, c=None):
        x = self.x if x is None else x
        y = self.y if y is None else y
        z = self.z if z is None else z
        c = self.c if c is None else c
        return {"seq": (y * 2 + x // 2) * 4 + z, "dp": (x % 2) * 2 + c}

    def peer(self, q):
        return {"seq": q, "dp": self.d}

    def sibling(self):
        return {"seq": self.q, "dp": self.d + 1 - 2 * self.c}

    def extra_of(self, e):
        return 8 * e + ((e + self.d // 2) % 2) * 4 + (e + self.d) % 4

    def has_extra(self):
        return self.q == self.extra_of(self.y)


def remote(src, dst, send, recv, device):
    return pltpu.make_async_remote_copy(
        src_ref=src, dst_ref=dst, send_sem=send, recv_sem=recv,
        device_id=device, device_id_type=MESH,
    )


def drain(ref, sem):
    pltpu.make_async_copy(ref, ref, sem).wait()


def greet(devices):
    barrier = pltpu.get_barrier_semaphore()
    for device in devices:
        pl.semaphore_signal(barrier, inc=1, device_id=device, device_id_type=MESH)
    return len(devices)


def greet_seq(here):
    barrier = pltpu.get_barrier_semaphore()

    def body(i, carry):
        pl.semaphore_signal(
            barrier, inc=1, device_id=here.peer((here.q + i) % 32), device_id_type=MESH
        )
        return carry

    lax.fori_loop(1, 32, body, 0)
    return 31


def rows(start, size):
    return pl.ds(pl.multiple_of(start * size, size), size)


TN = (((0,), (0,)), ((), ()))
NT = (((1,), (1,)), ((), ()))
NN = (((1,), (0,)), ((), ()))


def dot(a, b, dims):
    return lax.dot_general(a, b, dims, preferred_element_type=F32)


def lanes(start, size):
    return pl.ds(pl.multiple_of(start, LANES), size)


def block_of(ref, s, b):
    return ref.at[pl.ds(2 * s, 2), :, :, lanes(b * LANES, LANES)]


def column(ref, q, slot):
    return ref.at[pl.ds(2 * q, 2), :, :, pl.ds(slot * LANES, LANES)]


class ToChannels:
    def __init__(self, here, src, cols, sems):
        self.here, self.src, self.cols = here, src, cols
        self.send, self.recv, self.esend, self.erecv = sems

        @pl.when(jnp.logical_not(here.has_extra()))
        def _():
            cols[:, :, :, LANES:] = jnp.zeros((64, 2, 16, LANES), BF)

    def start(self, half):
        here, src, cols = self.here, self.src, self.cols
        first, count = ((0, 18), (18, 14))[half]

        def body(i, carry):
            dest = first + (i + here.q) % count
            block, place = block_of(src, dest // 6, dest % 6), column(cols, here.q, 0)

            @pl.when(dest != here.q)
            def _():
                remote(block, place, self.send, self.recv, here.peer(dest)).start()

            @pl.when(dest == here.q)
            def _():
                pltpu.make_async_copy(block, place, self.recv).start()

            return carry

        lax.fori_loop(0, count, body, 0)
        if half == 1:
            for e in range(4):
                dest = here.extra_of(e)
                block, place = block_of(src, 5, 2 + e), column(cols, here.q, 1)

                @pl.when(dest != here.q)
                def _():
                    remote(block, place, self.esend.at[e], self.erecv, here.peer(dest)).start()

                @pl.when(dest == here.q)
                def _():
                    pltpu.make_async_copy(block, place, self.erecv).start()

    def arrive(self):
        drain(self.cols.at[:, :, :, pl.ds(0, LANES)], self.recv)

        @pl.when(self.here.has_extra())
        def _():
            drain(self.cols.at[:, :, :, pl.ds(LANES, LANES)], self.erecv)

    def finish(self):
        drain(self.cols.at[pl.ds(0, 62), :, :, pl.ds(0, LANES)], self.send)
        for e in range(4):
            @pl.when(self.here.extra_of(e) != self.here.q)
            def _():
                drain(self.cols.at[pl.ds(0, 2), :, :, pl.ds(0, LANES)], self.esend.at[e])


class ToPatches:
    def __init__(self, here, cols, out, sems):
        self.here, self.cols, self.out = here, cols, out
        self.send, self.recv, self.esend = sems

    def start(self, dest):
        here, cols, out = self.here, self.cols, self.out
        place = block_of(out, here.q // 6, here.q % 6)
        extra = block_of(out, 5, 2 + here.y)
        sem = self.recv.at[here.q // 18]

        @pl.when(dest != here.q)
        def _():
            remote(column(cols, dest, 0), place, self.send, sem, here.peer(dest)).start()

            @pl.when(here.has_extra())
            def _():
                remote(
                    column(cols, dest, 1), extra, self.esend, self.recv.at[1], here.peer(dest)
                ).start()

        @pl.when(dest == here.q)
        def _():
            pltpu.make_async_copy(column(cols, dest, 0), place, sem).start()

            @pl.when(here.has_extra())
            def _():
                pltpu.make_async_copy(column(cols, dest, 1), extra, self.recv.at[1]).start()

    def arrive(self, half):
        drain(self.out.at[pl.ds(6 * half, 6)], self.recv.at[half])

    def finish(self):
        many = self.cols.at[pl.ds(0, 62), :, :, pl.ds(0, LANES)]
        drain(many, self.send)

        @pl.when(self.here.has_extra())
        def _():
            drain(many, self.esend)


class Gather:
    def __init__(self, here, parts, fulls, sems):
        self.here, self.fulls, self.parts = here, fulls, parts
        self.own, self.send, self.recv, self.bsend, self.brecv = sems
        self.copies = []
        self.legs = [{}, {}]
        c, y, xh, z = here.c, here.y, here.xh, here.z
        self.locals = []
        for w in range(2):
            copy = pltpu.make_async_copy(parts[w], fulls[w].at[y, xh, z], self.own.at[w])
            copy.start()
            self.locals.append(copy)
            self.push(w, 0, fulls[w].at[y, xh, z, c], here.at(x=(here.x + 2) % 4), parts[w].at[c])

    def piece(self, w, first, second, c, half=None):
        here = self.here
        y = (here.y + c * first + (1 - c) * second) % 4
        z = (here.z + (1 - c) * first + c * second) % 4
        h = slice(None) if half is None else half
        return self.fulls[w].at[y, h, z, c]

    def towards(self, axis, step):
        here = self.here
        along_y = here.c if axis == 0 else 1 - here.c
        return here.at(y=(here.y + along_y * step) % 4, z=(here.z + (1 - along_y) * step) % 4)

    def push(self, w, k, ref, device, src=None):
        copy = remote(
            ref if src is None else src, ref, self.send.at[w, k], self.recv.at[w, k], device
        )
        copy.start()
        self.copies.append(copy)
        self.legs[w][k] = copy

    def share(self, w, k, ref):
        copy = remote(ref, ref, self.bsend.at[w, k], self.brecv.at[w, k], self.here.sibling())
        copy.start()
        self.copies.append(copy)

    def around(self, w, ks, half, src=None):
        ref = self.piece(w, 0, 0, self.here.c, half)
        for k, axis, step in zip(ks, (0, 0, 1, 1), (1, 3, 1, 3)):
            self.push(w, k, ref, self.towards(axis, step), src)

    def launch(self, w):
        self.around(w, (1, 2, 5, 6), self.here.xh, self.parts[w].at[self.here.c])

    def crossed(self, w):
        here = self.here
        self.legs[w][0].wait_recv()
        self.around(w, (21, 22, 23, 24), 1 - here.xh)
        self.share(w, 0, self.piece(w, 0, 0, here.c, 1 - here.xh))
        self.locals[w].wait()

    def second(self, w, o):
        ref = self.piece(w, o, 0, self.here.c)
        self.push(w, 5 + 4 * o, ref, self.towards(1, 1))
        self.push(w, 6 + 4 * o, ref, self.towards(1, 3))

    def first_near(self, w):
        c = self.here.c
        self.legs[w][1].wait_recv()
        self.legs[w][21].wait_recv()
        self.push(w, 3, self.piece(w, 3, 0, c, 0), self.towards(0, 1))
        self.second(w, 3)
        self.share(w, 1, self.piece(w, 3, 0, c))
        self.legs[w][2].wait_recv()
        self.legs[w][22].wait_recv()
        self.push(w, 4, self.piece(w, 1, 0, c, 1), self.towards(0, 3))
        self.second(w, 1)
        self.share(w, 2, self.piece(w, 1, 0, c))

    def first_far(self, w):
        self.legs[w][3].wait_recv()
        self.legs[w][4].wait_recv()
        self.second(w, 2)
        self.share(w, 3, self.piece(w, 2, 0, self.here.c))

    def second_near(self, w, o):
        c = self.here.c
        self.legs[w][5 + 4 * o].wait_recv()
        if o == 0:
            self.legs[w][23].wait_recv()
        self.push(w, 7 + 4 * o, self.piece(w, o, 3, c, 0), self.towards(1, 1))
        self.share(w, 4 + 3 * o, self.piece(w, o, 3, c))
        self.legs[w][6 + 4 * o].wait_recv()
        if o == 0:
            self.legs[w][24].wait_recv()
        self.push(w, 8 + 4 * o, self.piece(w, o, 1, c, 1), self.towards(1, 3))
        self.share(w, 5 + 3 * o, self.piece(w, o, 1, c))

    def second_far(self, w, o):
        self.legs[w][7 + 4 * o].wait_recv()
        self.legs[w][8 + 4 * o].wait_recv()
        self.share(w, 6 + 3 * o, self.piece(w, o, 2, self.here.c))

    def shared_near(self, w):
        other = 1 - self.here.c
        drain(self.piece(w, 0, 0, other, 1 - self.here.xh), self.brecv.at[w, 0])
        for k, o in ((1, 3), (2, 1), (3, 2)):
            drain(self.piece(w, o, 0, other), self.brecv.at[w, k])
        for o in range(4):
            drain(self.piece(w, o, 3, other), self.brecv.at[w, 4 + 3 * o])
            drain(self.piece(w, o, 1, other), self.brecv.at[w, 5 + 3 * o])

    def shared_far(self, w):
        for o in range(4):
            drain(self.piece(w, o, 2, 1 - self.here.c), self.brecv.at[w, 6 + 3 * o])

    def finish(self):
        for copy in self.copies:
            copy.wait_send()


def add_into(target, *others):
    lead = target.shape[:-2]

    def body(i, carry):
        index = []
        rest = i
        for size in reversed(lead):
            index.append(rest % size)
            rest = rest // size
        index = tuple(reversed(index))
        total = target[index].astype(F32)
        for other in others:
            total += other[index].astype(F32)
        target[index] = total.astype(BF)
        return carry

    lax.fori_loop(0, math.prod(lead), body, 0, unroll=min(8, math.prod(lead)))


PARTS = (
    ("x", 48, 128), ("y", 48, 128), ("z", 48, 128),
    ("y", 16, 384), ("z", 16, 384), ("x", 16, 256),
    ("y", 16, 256), ("z", 16, 384), ("x", 16, 384),
)
PLANES = {"x": ("y", "z"), "y": ("z", "x"), "z": ("x", "y")}


class PartSum:
    def __init__(self, here, p, acc, bufs, send, recv):
        self.here, self.p, self.acc = here, p, acc
        self.low, self.high, self.up_buf, self.down_buf, self.turn_buf, self.end_buf = bufs
        self.send, self.recv = send, recv
        self.copies = []
        self.axis = PARTS[p][0]
        self.me = getattr(here, self.axis)

    def index(self, at):
        full = slice(None)
        if "x" in at:
            return (at.get("y", full), at["x"] // 2, at.get("z", full), at["x"] % 2)
        return (at.get("y", full), full, at.get("z", full), full)

    def chunk(self, pos, half=None):
        index = list(self.index({self.axis: pos}))
        if half is not None:
            if self.axis == "y":
                index[1] = half
            else:
                index[0] = pl.ds(2 * half, 2)
        return self.acc.at[tuple(index)]

    def to(self, step):
        return self.here.at(**{self.axis: (self.me + step) % 4})

    def push(self, k, src, dst, device):
        copy = remote(src, dst, self.send.at[self.p, k], self.recv.at[self.p, k], device)
        copy.start()
        self.copies.append(copy)
        return copy

    def begin(self):
        far = (self.me + 2) % 4
        self.legs = (
            self.push(0, self.chunk(far, 0), self.low, self.to(1)),
            self.push(1, self.chunk(far, 1), self.high, self.to(3)),
        )

    def relay(self):
        up, down = (self.me + 1) % 4, (self.me + 3) % 4
        self.legs[0].wait_recv()
        add_into(self.chunk(up, 0), self.low)
        one = self.push(2, self.chunk(up), self.up_buf, self.to(1))
        self.legs[1].wait_recv()
        add_into(self.chunk(down, 1), self.high)
        two = self.push(3, self.chunk(down), self.down_buf, self.to(3))
        self.legs = (one, two)

    def across(self, k, name, buf, at):
        me = getattr(self.here, name)
        for step in (1, 3, 2):
            pos = (me + step) % 4
            remote(
                self.acc.at[self.index({**at, name: pos})], buf.at[me],
                self.send.at[self.p, k], self.recv.at[self.p, k], self.here.at(**{name: pos}),
            ).start()

    def cross(self):
        self.legs[0].wait_recv()
        self.legs[1].wait_recv()
        add_into(self.chunk(self.me), self.up_buf, self.down_buf)
        self.across(4, PLANES[self.axis][0], self.turn_buf, {self.axis: self.me})

    def turn(self):
        a, b = PLANES[self.axis]
        me = getattr(self.here, a)
        at = {self.axis: self.me, a: me}
        drain(self.turn_buf.at[pl.ds(0, 3)], self.recv.at[self.p, 4])
        add_into(
            self.acc.at[self.index(at)], *[self.turn_buf.at[(me + k) % 4] for k in (1, 2, 3)]
        )
        self.across(5, b, self.end_buf, at)

    def end(self):
        a, b = PLANES[self.axis]
        me = getattr(self.here, b)
        at = {self.axis: self.me, a: getattr(self.here, a), b: me}
        drain(self.end_buf.at[pl.ds(0, 3)], self.recv.at[self.p, 5])
        total = self.acc[self.index(at)].astype(F32)
        for k in (1, 2, 3):
            total += self.end_buf[(me + k) % 4].astype(F32)
        return total

    def finish(self):
        for copy in self.copies:
            copy.wait_send()
        drain(self.turn_buf.at[pl.ds(0, 3)], self.send.at[self.p, 4])
        drain(self.end_buf.at[pl.ds(0, 3)], self.send.at[self.p, 5])


def part_shape(p):
    return (4, 2, 4, 2) + PARTS[p][1:]


def part_buffers(p):
    axis, tail = PARTS[p][0], PARTS[p][1:]
    whole = {"x": (4, 4), "y": (2, 4, 2), "z": (4, 2, 2)}[axis]
    half = whole[1:] if axis == "y" else (2,) + whole[1:]
    last = (2, 2) if PLANES[axis][1] == "x" else (4,)
    shapes = [half + tail] * 2 + [whole + tail] * 2 + [(4,) + last + tail, (4,) + tail]
    return [pltpu.VMEM(s, BF) for s in shapes]


DMA = pltpu.SemaphoreType.DMA
SCRATCH = dict(
    spectra=((384, 768), BF), cot=((384, 768), BF), grad_input=((384, 768), BF),
    win=((4, 2, 4, 2, 32, 1024), BF), wout=((4, 2, 4, 2, 32, 1024), BF),
    chin=((1536, 768), BF), chout=((1536, 768), BF),
    normed=((12, 2, 16, 768), BF), tm=((12, 2, 16, 768), BF), ng=((12, 2, 16, 768), BF),
    mixg=((12, 2, 16, 768), BF), ns=((384, 768), BF), mg=((384, 768), F32),
    cact=((384, 1536), BF), cgrad=((384, 1536), BF),
    cact_s=((384, 1536), BF), cgrad_s=((384, 1536), BF),
    ns_s=((384, 384), BF), cot_s=((384, 384), BF),
    cols_t=((256, 2048), BF), second=((192, 768), F32), down=((384, 1536), F32),
    cols=((64, 2, 16, 256), BF), cols2=((64, 2, 16, 256), BF),
    cols_s=((64, 16, 256), BF), cols2_s=((64, 16, 256), BF),
    hidden=((256, 1024), F32), slope=((256, 1024), F32),
    act=((256, 1024), BF), act_s=((256, 1024), BF),
    hg=((256, 1024), BF), hg_s=((256, 1024), BF),
    mixb=((64, 2, 16, 256), BF), ncg=((64, 2, 16, 256), BF),
    fin=((4, 48, 384), F32), sum0=((16, 1024), F32), sum1=((16, 1024), F32),
    sum2=((12, 768), F32), sum3=((12, 768), F32),
)
SEMS = dict(
    load=(5,), a1_send=(), a1_recv=(), a1_esend=(4,), a1_erecv=(),
    a3_send=(), a3_recv=(), a3_esend=(4,), a3_erecv=(),
    a2_send=(), a2_recv=(2,), a2_esend=(),
    a4_send=(), a4_recv=(2,), a4_esend=(),
    w_own=(2,), w_send=(2, 25), w_recv=(2, 25), w_bsend=(2, 16), w_brecv=(2, 16),
    r_send=(9, 6), r_recv=(9, 6),
    s_send=(11,), s_recv=(11,), f_send=(3,), f_recv=(3,),
)


def block_kernel(
    spectra_in, cot_in, w_in, w_out, ch_in, ch_out, grad_out, o0, o1, o2, o3, *scratch
):
    v = types.SimpleNamespace(**dict(zip(list(SCRATCH) + list(SEMS), scratch)))
    spectra, cot, grad_input = v.spectra, v.cot, v.grad_input
    bufs = scratch[len(SCRATCH) + len(SEMS):]
    sums = scratch[len(SCRATCH) + len(SEMS) + 6 * len(PARTS):]
    here = Here()
    c = here.c
    sib = here.sibling()
    cross = here.at(x=here.xh * 2 + 1 - here.xl, c=1 - c)
    partners = [sib, cross]
    for k in (1, 3):
        x = (here.x + k) % 4
        partners += [here.at(x=x, z=(here.z + n) % 4) for n in range(4)]
        partners += [here.at(x=x, y=(here.y + n) % 4) for n in range(1, 4)]
    count = greet_seq(here) + greet(partners)
    loads = [
        pltpu.make_async_copy(src, dst, v.load.at[k])
        for k, (src, dst) in enumerate((
            (spectra_in, spectra), (cot_in, cot), (ch_in, v.chin), (ch_out, v.chout),
        ))
    ]
    for copy in loads:
        copy.start()
    loads.pop(0).wait()

    def norm_first(i, carry):
        unit, _ = normalize(spectra[rows(i, 32), :].astype(F32))
        v.normed[i] = unit.astype(BF).reshape(2, 16, 768)
        return carry

    lax.fori_loop(0, 12, norm_first, 0, unroll=6)
    pl.semaphore_wait(pltpu.get_barrier_semaphore(), count)

    shared = []

    def share(src, dst):
        k = len(shared)
        copy = remote(src, dst, v.s_send.at[k], v.s_recv.at[k], sib)
        copy.start()
        shared.append(copy)
        return copy

    gather = Gather(
        here, (w_in, w_out), (v.win, v.wout),
        (v.w_own, v.w_send, v.w_recv, v.w_bsend, v.w_brecv),
    )
    first = ToChannels(
        here, v.normed, v.cols, (v.a1_send, v.a1_recv, v.a1_esend, v.a1_erecv)
    )
    both = range(2)
    for w in both:
        gather.launch(w)
    first.start(0)
    first.start(1)
    for w in both:
        gather.crossed(w)
    for copy in loads:
        copy.wait()
    share(cot.at[:, lanes(384 * (1 - c), 384)], v.cot_s)

    def channel_down(i, carry):
        v.down[:, lanes(256 * i, 256)] = dot(cot[...], v.chout[rows(i, 256), :], NT)
        return carry

    for w in both:
        gather.first_near(w)
    lax.fori_loop(0, 3, channel_down, 0)
    for w in both:
        gather.second_near(w, 0)
    for w in both:
        gather.first_far(w)
    lax.fori_loop(3, 6, channel_down, 0)
    for o in (3, 1):
        for w in both:
            gather.second_near(w, o)
    first.arrive()
    share(v.cols.at[:, 1 - c], v.cols_s)
    for w in both:
        gather.second_near(w, 2)

    def turn_cols(y, carry):
        v.cols_t[:, lanes(512 * y, 512)] = v.cols[pl.ds(16 * y, 16)].reshape(512, 256).T
        return carry

    lax.fori_loop(0, 4, turn_cols, 0, unroll=2)
    for o in (0, 3, 1, 2):
        gather.second_far(0, o)
    gather.shared_near(0)
    gather.shared_far(0)

    def project(source, weight):
        def step(y, start):
            left = source[pl.ds(16 * y, 16)].reshape(512, 256)
            part = dot(left, weight[y].reshape(512, 1024), TN)
            if start:
                v.hidden[...] = part
            else:
                v.hidden[...] += part

        step(0, True)
        for y in range(1, 4):
            step(y, False)

    def hidden_of(i, carry):
        part = lanes(256 * i, 256)
        weight = v.win[:, :, :, :, :, part].reshape(2048, 256)
        v.hidden[:, part] = dot(v.cols_t[...], weight, NN)
        return carry

    lax.fori_loop(0, 4, hidden_of, 0, unroll=4)

    def token_gelu(i, carry):
        at = rows(i, 16)
        value, slope = gelu_pair(v.hidden[at, :])
        v.act[at, :] = value.astype(BF)
        v.slope[at, :] = slope
        return carry

    lax.fori_loop(0, 16, token_gelu, 0, unroll=8)
    share(v.act, v.act_s)

    def spread(weight, source, target, transfer, spots):
        left = jnp.concatenate([weight[y, :, z].reshape(128, 1024) for y, z in spots], axis=0)
        value = dot(left, source[...], NT).astype(BF).reshape(len(spots), 2, 2, 2, 16, 256)
        for k, (y, z) in enumerate(spots):
            for xh in range(2):
                dest = 8 * y + 4 * xh + z
                target[pl.ds(2 * dest, 2)] = value[k, xh]
                transfer.start(dest)

    def off(name, step):
        return (getattr(here, name) + step) % 4

    second = ToPatches(
        here, v.mixb, v.tm, (v.a2_send, v.a2_recv, v.a2_esend)
    )
    gather.shared_near(1)

    def near(i, carry):
        z = off("z", i + i // 2)
        spread(
            v.wout, v.act, v.mixb, second, [(off("y", step), z) for step in (1, 3, 0)]
        )
        return carry

    lax.fori_loop(0, 3, near, 0)
    for o in (0, 3, 1, 2):
        gather.second_far(1, o)
    gather.shared_far(1)
    spread(
        v.wout, v.act, v.mixb, second,
        [(off("y", 2), off("z", step)) for step in (1, 3, 0)],
    )
    spread(
        v.wout, v.act, v.mixb, second,
        [(off("y", step), off("z", 2)) for step in (2, 1, 3, 0)],
    )
    gather.finish()
    first.finish()

    third = ToChannels(
        here, v.mixg, v.cols2, (v.a3_send, v.a3_recv, v.a3_esend, v.a3_erecv)
    )

    def middle_of(at):
        source = spectra[rows(at, 32), :].astype(F32)
        mix = v.tm[at].reshape(32, 768).astype(F32)
        return (source + mix).astype(BF).astype(F32)

    for half in range(2):
        second.arrive(half)
        span = pl.ds(192 * half, 192)

        def norm_second(i, carry):
            at = half * 6 + i
            v.ns[rows(at, 32), :] = normalize(middle_of(at))[0].astype(BF)
            return carry

        lax.fori_loop(0, 6, norm_second, 0, unroll=6)

        def hidden_units(i, carry):
            part = lanes(256 * i, 256)
            own = rows(i, 256)
            value, slope = gelu_pair(dot(v.ns[span, :], v.chin[own, :], NT))
            v.cact[span, part] = value.astype(BF)
            v.cgrad[span, part] = (v.down[span, part] * slope).astype(BF)
            return carry

        lax.fori_loop(0, 6, hidden_units, 0, unroll=3)
        for src, dst in ((v.cgrad, v.cgrad_s), (v.cact, v.cact_s)):
            share(src.at[span], dst.at[span])
        share(v.ns.at[span, lanes(384 * (1 - c), 384)], v.ns_s.at[span])
        v.second[...] = dot(v.cgrad[span, :], v.chin[...], NN)

        def back_second(i, carry):
            at = half * 6 + i
            unit, scale = normalize(middle_of(at))
            upstream = v.second[rows(i, 32), :]
            value = cot[rows(at, 32), :].astype(F32) + norm_back(unit, scale, upstream)
            v.mg[rows(at, 32), :] = value
            v.mixg[at] = value.astype(BF).reshape(2, 16, 768)
            return carry

        lax.fori_loop(0, 6, back_second, 0, unroll=6)
        third.start(half)

    for copy in shared:
        copy.wait_recv()
    half_lanes = lanes(384 * c, 384)
    for g, (act, tok, act_s, tok_s) in enumerate((
        (v.cgrad, v.ns, v.cgrad_s, v.ns_s), (v.cact, cot, v.cact_s, v.cot_s),
    )):
        def channel_sum(y, carry):
            part = lanes(384 * y, 384)
            total = dot(act[:, part], tok[:, half_lanes], TN)
            total += dot(act_s[:, part], tok_s[...], TN)
            total = total.astype(BF).reshape(2, 4, 48, 384)
            for p in range(3):
                sums[p][y, :, :, g] = total[..., 128 * p:128 * p + 128]
            return carry

        lax.fori_loop(0, 4, channel_sum, 0, unroll=4)

    parts = [
        PartSum(here, p, sums[p], bufs[6 * p:6 * p + 6], v.r_send, v.r_recv)
        for p in range(len(PARTS))
    ]
    channel_parts, early, late = parts[:3], parts[3:6], parts[6:]
    for part in channel_parts:
        part.begin()
    for part in channel_parts:
        part.relay()

    second.finish()
    third.arrive()
    share_cols2 = share(v.cols2.at[:, 1 - c], v.cols2_s)
    project(v.cols2, v.wout)

    def token_grad(i, carry):
        at = rows(i, 16)
        v.hg[at, :] = (v.hidden[at, :] * v.slope[at, :]).astype(BF)
        return carry

    lax.fori_loop(0, 16, token_grad, 0, unroll=8)
    share_hg = share(v.hg, v.hg_s)

    def token_sum(left, left_s, right, right_s, targets):
        def step(y, carry):
            own = left[pl.ds(16 * y, 16), c].reshape(256, 256)
            other = left_s[pl.ds(16 * y, 16)].reshape(256, 256)
            total = dot(own, right[...], NN) + dot(other, right_s[...], NN)
            total = total.astype(BF).reshape(2, 4, 2, 16, 1024)
            place = 0
            for p in targets:
                width = PARTS[p][2]
                sums[p][y] = total[..., place:place + width]
                place += width
            return carry

        lax.fori_loop(0, 4, step, 0, unroll=4)

    share_cols2.wait_recv()
    token_sum(
        v.cols2, v.cols2_s, v.act, v.act_s, (3, 4, 5),
    )
    for part in early:
        part.begin()
    for part in channel_parts:
        part.cross()
    share_hg.wait_recv()
    token_sum(
        v.cols, v.cols_s, v.hg, v.hg_s, (6, 7, 8),
    )
    for part in late:
        part.begin()
    for part in early:
        part.relay()
    for part in channel_parts:
        part.turn()
    fourth = ToPatches(
        here, v.ncg, v.ng, (v.a4_send, v.a4_recv, v.a4_esend)
    )

    def back(i, carry):
        z = off("z", 3 - i)
        spread(
            v.win, v.hg, v.ncg, fourth, [(off("y", step), z) for step in (2, 1, 3, 0)]
        )
        return carry

    lax.fori_loop(0, 4, back, 0, unroll=2)
    for part in late:
        part.relay()
    for part in early:
        part.cross()

    def input_grad(half):
        fourth.arrive(half)

        def step(i, carry):
            at = half * 6 + i
            unit, scale = normalize(spectra[rows(at, 32), :].astype(F32))
            upstream = v.ng[at].reshape(32, 768).astype(F32)
            value = v.mg[rows(at, 32), :] + norm_back(unit, scale, upstream)
            grad_input[rows(at, 32), :] = value.astype(BF)
            return carry

        lax.fori_loop(0, 6, step, 0, unroll=6)

    for p, part in enumerate(channel_parts):
        v.fin[here.d, :, 128 * p:128 * p + 128] = part.end()
    input_grad(0)
    swaps = []
    for k, device in enumerate((sib, here.at(x=here.xh * 2 + 1 - here.xl), cross)):
        copy = remote(
            v.fin.at[here.d], v.fin.at[here.d], v.f_send.at[k], v.f_recv.at[k], device
        )
        copy.start()
        swaps.append(copy)
    for part in early:
        part.turn()
    for part in late:
        part.cross()
    input_grad(1)
    stores = [pltpu.make_async_copy(grad_input, grad_out, v.load.at[4])]
    stores[0].start()
    for part in late:
        part.turn()

    def gather_up(out, group):
        place = 0
        for part in group:
            width = PARTS[part.p][2]
            out[:, place:place + width] = part.end()
            place += width

    def keep(k, src, dst):
        copy = pltpu.make_async_copy(src, dst, v.load.at[k])
        copy.start()
        return copy

    gather_up(v.sum1, early)
    stores.append(keep(0, v.sum1, o1))
    for copy in swaps:
        copy.wait()
    for d in range(4):
        @pl.when(here.d == d)
        def _():
            for total, g in ((v.sum2, 0), (v.sum3, 2)):
                for k in range(2):
                    total[:, 384 * k:384 * k + 384] = v.fin[g + k, 12 * d:12 * d + 12]
    stores.append(keep(1, v.sum2, o2))
    stores.append(keep(2, v.sum3, o3))
    for part in channel_parts + early:
        part.finish()
    for copy in shared:
        copy.wait_send()
    third.finish()
    fourth.finish()
    gather_up(v.sum0, late)
    stores.append(keep(3, v.sum0, o0))
    for part in late:
        part.finish()
    for copy in stores:
        copy.wait()


def hand_over(*refs):
    for src, dst in zip(refs[:5], refs[5:]):
        dst[...] = src[...]


def local(spectra_in, cotangent, tok_in_w, tok_out_w, ch_in_w, ch_out_w):
    vmem = pl.BlockSpec(memory_space=pltpu.VMEM)
    scratch = [pltpu.VMEM(shape, kind) for shape, kind in SCRATCH.values()]
    scratch += [DMA(shape) if shape else DMA for shape in SEMS.values()]
    for p in range(len(PARTS)):
        scratch += part_buffers(p)
    scratch += [pltpu.VMEM(part_shape(p), BF) for p in range(len(PARTS))]
    shapes = (
        jax.ShapeDtypeStruct((384, 768), BF),
        jax.ShapeDtypeStruct((16, 1024), F32),
        jax.ShapeDtypeStruct((16, 1024), F32),
        jax.ShapeDtypeStruct((12, 768), F32),
        jax.ShapeDtypeStruct((12, 768), F32),
    )
    outs = pl.pallas_call(
        block_kernel,
        out_shape=shapes,
        in_specs=[ANY] * 6, out_specs=(ANY,) * 5,
        scratch_shapes=scratch,
        compiler_params=pltpu.CompilerParams(
            collective_id=0, has_side_effects=True, vmem_limit_bytes=60 * 1024 * 1024
        ),
        name="mixer_block_backward",
    )(
        spectra_in.reshape(384, 768), cotangent.reshape(384, 768),
        tok_in_w.reshape(2, 32, 1024), tok_out_w.reshape(2, 32, 1024), ch_in_w, ch_out_w,
    )
    grad_input, *weights = pl.pallas_call(
        hand_over, out_shape=shapes, in_specs=[vmem] * 5, out_specs=(vmem,) * 5, name="hand_over",
    )(*outs)
    return (grad_input.reshape(6, 64, 768), *weights)


def solution(mesh):
    in_specs = (
        P("dp", "seq", None),
        P("dp", "seq", None),
        P("seq", None),
        P("seq", None),
        P(),
        P(),
    )
    out_specs = (
        P("dp", "seq", None),
        P(("seq", "dp"), None),
        P(("seq", "dp"), None),
        P(("seq", "dp"), None),
        P(("seq", "dp"), None),
    )
    return jax.shard_map(local, mesh=mesh, in_specs=in_specs, out_specs=out_specs, check_vma=False)
```

profile of v0, /device:TPU:0, one launch (start us, length us, event | category | flops | bytes accessed | tf_op | source)
XLA Modules:
  0.0 122.2 jit_solution(1497913274581143088)
XLA Ops:
  0.6 119.6 %mixer_block_backward.1 = (bf16[384,768]{1,0:T(8,128)(2,1)}, f32[16,1024]{1,0:T(8,128)}, f32[16,1024]{1,0:T(8,128)}, f32[12,768]{1,0:T(8,128)}, f32[12,768]{1,0:T(8,128)}) custom-call(bf16[384,768]{1,0:T(8,128)(2,1)} %bitcast.5, bf16[384,768]{1,0:T(8,128)(2,1)} %bitcast.6, bf16[2,32,1024]{2,1,0:T(8,128)(2,1)} %bitcast.7, bf16[2,32,1024]{2,1,0:T(8,128)(2,1)} %bitcast.8, ...), custom_call_target="tpu_custom_call" | custom-call | tf_op jit(solution)/shard_map/mixer_block_backward/pallas_call | solution.py:890
  120.2 2.0 %hand_over.1 = (bf16[384,768]{1,0:T(8,128)(2,1)}, f32[16,1024]{1,0:T(8,128)}, f32[16,1024]{1,0:T(8,128)}, f32[12,768]{1,0:T(8,128)}, f32[12,768]{1,0:T(8,128)}) custom-call(bf16[384,768]{1,0:T(8,128)(2,1)} %get-tuple-element.15.refs_0_, f32[16,1024]{1,0:T(8,128)} %get-tuple-element.16.refs_1_, f32[16,1024]{1,0:T(8,128)} %get-tuple-element.17.refs_2_, ...), custom_call_target="tpu_custom_call" | custom-call | tf_op jit(solution)/shard_map/hand_over/pallas_call | solution.py:903
where the time goes:
time: 122 us
  Pallas kernels  122 us (100%)
    pallas_call x1, Pallas kernels, local(): pl.pallas_call(block_kernel, out_shape=shapes, in_specs=[ANY] * 6, out_sp...  120 us

commit v1 on v0

--- a/solution.py
+++ b/solution.py
@@ -29,12 +29,10 @@
 
 def gelu_pair(values):
     factor = math.sqrt(2.0 / math.pi)
-    inner = factor * (values + 0.044715 * values * values * values)
-    tangent = jnp.tanh(inner)
-    result = 0.5 * values * (1.0 + tangent)
-    slope = 0.5 * (1.0 + tangent) + 0.5 * values * (1.0 - tangent * tangent) * factor * (
-        1.0 + 3.0 * 0.044715 * values * values
-    )
+    square = values * values
+    half = 0.5 + 0.5 * jnp.tanh(values * (factor + (factor * 0.044715) * square))
+    result = values * half
+    slope = half + result * (1.0 - half) * (2.0 * factor + (6.0 * factor * 0.044715) * square)
     return (result, slope)
 
 
@@ -470,6 +468,7 @@
 
 DMA = pltpu.SemaphoreType.DMA
 SCRATCH = dict(
+    scale_first=((384, 1), F32), scale_second=((384, 1), F32),
     spectra=((384, 768), BF), cot=((384, 768), BF), grad_input=((384, 768), BF),
     win=((4, 2, 4, 2, 32, 1024), BF), wout=((4, 2, 4, 2, 32, 1024), BF),
     chin=((1536, 768), BF), chout=((1536, 768), BF),
@@ -515,7 +514,6 @@
         x = (here.x + k) % 4
         partners += [here.at(x=x, z=(here.z + n) % 4) for n in range(4)]
         partners += [here.at(x=x, y=(here.y + n) % 4) for n in range(1, 4)]
-    count = greet_seq(here) + greet(partners)
     loads = [
         pltpu.make_async_copy(src, dst, v.load.at[k])
         for k, (src, dst) in enumerate((
@@ -524,11 +522,13 @@
     ]
     for copy in loads:
         copy.start()
+    count = greet_seq(here) + greet(partners)
     loads.pop(0).wait()
 
     def norm_first(i, carry):
-        unit, _ = normalize(spectra[rows(i, 32), :].astype(F32))
+        unit, scale = normalize(spectra[rows(i, 32), :].astype(F32))
         v.normed[i] = unit.astype(BF).reshape(2, 16, 768)
+        v.scale_first[rows(i, 32), :] = scale
         return carry
 
     lax.fori_loop(0, 12, norm_first, 0, unroll=6)
@@ -676,7 +676,9 @@
 
         def norm_second(i, carry):
             at = half * 6 + i
-            v.ns[rows(at, 32), :] = normalize(middle_of(at))[0].astype(BF)
+            unit, scale = normalize(middle_of(at))
+            v.ns[rows(at, 32), :] = unit.astype(BF)
+            v.scale_second[rows(at, 32), :] = scale
             return carry
 
         lax.fori_loop(0, 6, norm_second, 0, unroll=6)
@@ -697,7 +699,8 @@
 
         def back_second(i, carry):
             at = half * 6 + i
-            unit, scale = normalize(middle_of(at))
+            unit = v.ns[rows(at, 32), :].astype(F32)
+            scale = v.scale_second[rows(at, 32), :]
             upstream = v.second[rows(i, 32), :]
             value = cot[rows(at, 32), :].astype(F32) + norm_back(unit, scale, upstream)
             v.mg[rows(at, 32), :] = value
@@ -802,7 +805,8 @@
 
         def step(i, carry):
             at = half * 6 + i
-            unit, scale = normalize(spectra[rows(at, 32), :].astype(F32))
+            unit = v.normed[at].reshape(32, 768).astype(F32)
+            scale = v.scale_first[rows(at, 32), :]
             upstream = v.ng[at].reshape(32, 768).astype(F32)
             value = v.mg[rows(at, 32), :] + norm_back(unit, scale, upstream)
             grad_input[rows(at, 32), :] = value.astype(BF)

time: 122 us -> 122 us (level)
  no operation moved by 1% of the time
where the time goes in v1:
time: 122 us
  Pallas kernels  121 us (99%)
    pallas_call x1, Pallas kernels, local(): pl.pallas_call(block_kernel, out_shape=shapes, in_specs=[ANY] * 6, out_sp...  119 us

profile of v1, /device:TPU:0, one launch (start us, length us, event | category | flops | bytes accessed | tf_op | source)
XLA Modules:
  0.0 121.8 jit_solution(12847128350114270474)
XLA Ops:
  0.6 119.2 %mixer_block_backward.1 = (bf16[384,768]{1,0:T(8,128)(2,1)}, f32[16,1024]{1,0:T(8,128)}, f32[16,1024]{1,0:T(8,128)}, f32[12,768]{1,0:T(8,128)}, f32[12,768]{1,0:T(8,128)}) custom-call(bf16[384,768]{1,0:T(8,128)(2,1)} %bitcast.5, bf16[384,768]{1,0:T(8,128)(2,1)} %bitcast.6, bf16[2,32,1024]{2,1,0:T(8,128)(2,1)} %bitcast.7, bf16[2,32,1024]{2,1,0:T(8,128)(2,1)} %bitcast.8, ...), custom_call_target="tpu_custom_call" | custom-call | tf_op jit(solution)/shard_map/mixer_block_backward/pallas_call | solution.py:894
  119.8 2.0 %hand_over.1 = (bf16[384,768]{1,0:T(8,128)(2,1)}, f32[16,1024]{1,0:T(8,128)}, f32[16,1024]{1,0:T(8,128)}, f32[12,768]{1,0:T(8,128)}, f32[12,768]{1,0:T(8,128)}) custom-call(bf16[384,768]{1,0:T(8,128)(2,1)} %get-tuple-element.15.refs_0_, f32[16,1024]{1,0:T(8,128)} %get-tuple-element.16.refs_1_, f32[16,1024]{1,0:T(8,128)} %get-tuple-element.17.refs_2_, ...), custom_call_target="tpu_custom_call" | custom-call | tf_op jit(solution)/shard_map/hand_over/pallas_call | solution.py:907

commit v2 on v1

--- a/solution.py
+++ b/solution.py
@@ -184,14 +184,13 @@
         self.here, self.cols, self.out = here, cols, out
         self.send, self.recv, self.esend = sems
 
-    def start(self, dest):
+    def start(self, dest, other):
         here, cols, out = self.here, self.cols, self.out
         place = block_of(out, here.q // 6, here.q % 6)
         extra = block_of(out, 5, 2 + here.y)
         sem = self.recv.at[here.q // 18]
 
-        @pl.when(dest != here.q)
-        def _():
+        def away():
             remote(column(cols, dest, 0), place, self.send, sem, here.peer(dest)).start()
 
             @pl.when(here.has_extra())
@@ -199,6 +198,11 @@
                 remote(
                     column(cols, dest, 1), extra, self.esend, self.recv.at[1], here.peer(dest)
                 ).start()
+
+        if other:
+            away()
+            return
+        pl.when(dest != here.q)(away)
 
         @pl.when(dest == here.q)
         def _():
@@ -623,13 +627,13 @@
     share(v.act, v.act_s)
 
     def spread(weight, source, target, transfer, spots):
-        left = jnp.concatenate([weight[y, :, z].reshape(128, 1024) for y, z in spots], axis=0)
+        left = jnp.concatenate([weight[y, :, z].reshape(128, 1024) for y, z, _ in spots], axis=0)
         value = dot(left, source[...], NT).astype(BF).reshape(len(spots), 2, 2, 2, 16, 256)
-        for k, (y, z) in enumerate(spots):
+        for k, (y, z, other) in enumerate(spots):
             for xh in range(2):
                 dest = 8 * y + 4 * xh + z
                 target[pl.ds(2 * dest, 2)] = value[k, xh]
-                transfer.start(dest)
+                transfer.start(dest, other)
 
     def off(name, step):
         return (getattr(here, name) + step) % 4
@@ -642,7 +646,7 @@
     def near(i, carry):
         z = off("z", i + i // 2)
         spread(
-            v.wout, v.act, v.mixb, second, [(off("y", step), z) for step in (1, 3, 0)]
+            v.wout, v.act, v.mixb, second, [(off("y", step), z, step > 0) for step in (1, 3, 0)]
         )
         return carry
 
@@ -652,11 +656,11 @@
     gather.shared_far(1)
     spread(
         v.wout, v.act, v.mixb, second,
-        [(off("y", 2), off("z", step)) for step in (1, 3, 0)],
+        [(off("y", 2), off("z", step), True) for step in (1, 3, 0)],
     )
     spread(
         v.wout, v.act, v.mixb, second,
-        [(off("y", step), off("z", 2)) for step in (2, 1, 3, 0)],
+        [(off("y", step), off("z", 2), True) for step in (2, 1, 3, 0)],
     )
     gather.finish()
     first.finish()
@@ -790,7 +794,7 @@
     def back(i, carry):
         z = off("z", 3 - i)
         spread(
-            v.win, v.hg, v.ncg, fourth, [(off("y", step), z) for step in (2, 1, 3, 0)]
+            v.win, v.hg, v.ncg, fourth, [(off("y", step), z, step > 0) for step in (2, 1, 3, 0)]
         )
         return carry
 

time: 122 us -> 122 us (level)
  no operation moved by 1% of the time
where the time goes in v2:
time: 122 us
  Pallas kernels  121 us (99%)
    pallas_call x1, Pallas kernels, local(): pl.pallas_call(block_kernel, out_shape=shapes, in_specs=[ANY] * 6, out_sp...  119 us

profile of v2, /device:TPU:0, one launch (start us, length us, event | category | flops | bytes accessed | tf_op | source)
XLA Modules:
  0.0 121.6 jit_solution(9990509106862038092)
XLA Ops:
  0.6 119.0 %mixer_block_backward.1 = (bf16[384,768]{1,0:T(8,128)(2,1)}, f32[16,1024]{1,0:T(8,128)}, f32[16,1024]{1,0:T(8,128)}, f32[12,768]{1,0:T(8,128)}, f32[12,768]{1,0:T(8,128)}) custom-call(bf16[384,768]{1,0:T(8,128)(2,1)} %bitcast.5, bf16[384,768]{1,0:T(8,128)(2,1)} %bitcast.6, bf16[2,32,1024]{2,1,0:T(8,128)(2,1)} %bitcast.7, bf16[2,32,1024]{2,1,0:T(8,128)(2,1)} %bitcast.8, ...), custom_call_target="tpu_custom_call" | custom-call | tf_op jit(solution)/shard_map/mixer_block_backward/pallas_call | solution.py:898
  119.6 2.0 %hand_over.1 = (bf16[384,768]{1,0:T(8,128)(2,1)}, f32[16,1024]{1,0:T(8,128)}, f32[16,1024]{1,0:T(8,128)}, f32[12,768]{1,0:T(8,128)}, f32[12,768]{1,0:T(8,128)}) custom-call(bf16[384,768]{1,0:T(8,128)(2,1)} %get-tuple-element.15.refs_0_, f32[16,1024]{1,0:T(8,128)} %get-tuple-element.16.refs_1_, f32[16,1024]{1,0:T(8,128)} %get-tuple-element.17.refs_2_, ...), custom_call_target="tpu_custom_call" | custom-call | tf_op jit(solution)/shard_map/hand_over/pallas_call | solution.py:911

commit v3 on v2

--- a/solution.py
+++ b/solution.py
@@ -571,12 +571,10 @@
 
     for w in both:
         gather.first_near(w)
-    lax.fori_loop(0, 3, channel_down, 0)
     for w in both:
         gather.second_near(w, 0)
     for w in both:
         gather.first_far(w)
-    lax.fori_loop(3, 6, channel_down, 0)
     for o in (3, 1):
         for w in both:
             gather.second_near(w, o)
@@ -662,6 +660,7 @@
         v.wout, v.act, v.mixb, second,
         [(off("y", step), off("z", 2), True) for step in (2, 1, 3, 0)],
     )
+    lax.fori_loop(0, 6, channel_down, 0, unroll=2)
     gather.finish()
     first.finish()
 

time: 122 us -> 122 us (level)
  no operation moved by 1% of the time
where the time goes in v3:
time: 122 us
  Pallas kernels  121 us (99%)
    pallas_call x1, Pallas kernels, local(): pl.pallas_call(block_kernel, out_shape=shapes, in_specs=[ANY] * 6, out_sp...  119 us

profile of v3, /device:TPU:0, one launch (start us, length us, event | category | flops | bytes accessed | tf_op | source)
XLA Modules:
  0.0 121.6 jit_solution(17661890419746546410)
XLA Ops:
  0.6 119.0 %mixer_block_backward.1 = (bf16[384,768]{1,0:T(8,128)(2,1)}, f32[16,1024]{1,0:T(8,128)}, f32[16,1024]{1,0:T(8,128)}, f32[12,768]{1,0:T(8,128)}, f32[12,768]{1,0:T(8,128)}) custom-call(bf16[384,768]{1,0:T(8,128)(2,1)} %bitcast.5, bf16[384,768]{1,0:T(8,128)(2,1)} %bitcast.6, bf16[2,32,1024]{2,1,0:T(8,128)(2,1)} %bitcast.7, bf16[2,32,1024]{2,1,0:T(8,128)(2,1)} %bitcast.8, ...), custom_call_target="tpu_custom_call" | custom-call | tf_op jit(solution)/shard_map/mixer_block_backward/pallas_call | solution.py:897
  119.6 2.0 %hand_over.1 = (bf16[384,768]{1,0:T(8,128)(2,1)}, f32[16,1024]{1,0:T(8,128)}, f32[16,1024]{1,0:T(8,128)}, f32[12,768]{1,0:T(8,128)}, f32[12,768]{1,0:T(8,128)}) custom-call(bf16[384,768]{1,0:T(8,128)(2,1)} %get-tuple-element.15.refs_0_, f32[16,1024]{1,0:T(8,128)} %get-tuple-element.16.refs_1_, f32[16,1024]{1,0:T(8,128)} %get-tuple-element.17.refs_2_, ...), custom_call_target="tpu_custom_call" | custom-call | tf_op jit(solution)/shard_map/hand_over/pallas_call | solution.py:910
